TPU v7x, 32 devices: a whole 2x2x4 slice. The times are simulated.
32 devices in a mesh: groups: 2 (over y), tensor: 4 (over z), store: 4 (over x, core).
Axes of the slice: x: 2, y: 2, z: 4, core: 2. Of those that a mesh axis runs over, the one named last changes fastest.
Arguments:
- hidden_activations: bfloat16 [2048, 28672], P('groups', 'tensor'), parts along dimension 0, may hold values from -6 to 6
- down_matrix: bfloat16 [28672, 8192], P('tensor', 'store'), may hold values from -0.03125 to 0.03125
- adapter_input_factor: bfloat16 [32, 28672, 128], P(('groups', 'store'), 'tensor'), parts along dimension 0, may hold values from -0.03125 to 0.03125
- adapter_output_factor: bfloat16 [32, 128, 8192], P(('groups', 'store'), 'tensor'), parts along dimension 0, may hold values from -0.5 to 0.5
- token_requests: int32 [2048], P('groups'), parts along dimension 0, may hold values from 0 to 3, never falling along the last dimension, each value on 1 to 512 neighbouring positions
- request_adapters: int32 [8], P('groups'), parts along dimension 0, may hold values from 0 to 15
- adapter_ranks: int32 [32], P('groups'), parts along dimension 0, may hold values from 16 to 128, as said below
- adapter_store_slot: int32 [32], P('groups'), parts along dimension 0, may hold values from 0 to 15, each once
Outputs:
- mixed: bfloat16 [2048, 8192], P(('groups', 'tensor'), 'store'), parts along dimension 0
There are 2 independent parts, one for each index of `groups`. A program takes and returns all parts, laid end to end along the dimension named above; an argument that names none is the same for every part. Nothing has to cross between parts.
Inputs may be any that keep to these rules, and one draw needn't show every extreme that they name: `adapter_ranks`: each rank is 128, 64, 32 or 16; some adapter has rank 128.
All inputs are finite; a program needn't handle non-finite values.
Results may differ from a plain program's by a relative error of at most 0.013.
Values may be sent and summed in bfloat16 or wider, within the bound.
No kernel may reach another device: no remote copies, remote signals or barrier semaphores. Data moves between devices by JAX's collectives and lax.ppermute only.
A program may use at most 192 MiB of HBM per device.

v0:
```python
import functools

import jax
import jax.numpy as jnp
from jax import lax
from jax.experimental import pallas as pl
from jax.experimental.pallas import tpu as pltpu
from jax.sharding import PartitionSpec as P

LINE = 4
LANES = 128
AHEAD = 3
PAIRS = 2
MIB = 1024 * 1024


def line_order(n):
    order = []
    for z in range(n):
        sends = [(t, z >= n // 2, n - 1 - t + z) for t in range(z, n - 1)]
        sends += [(t, z < n // 2, t - (n - 1 - z)) for t in range(n - 1 - z, n - 1)]
        order.append([block for _, _, block in sorted(sends)] + [z])
    return order


def first_divisor(size, choices):
    for choice in choices:
        if size % choice == 0:
            return choice
    return size


def after(token, *done):
    return lax.optimization_barrier((token, done))[0]


def params(mebibytes):
    return pltpu.CompilerParams(vmem_limit_bytes=mebibytes * MIB)


def small_cost():
    return pl.CostEstimate(flops=10**6, bytes_accessed=10**5, transcendentals=0)


def block_at(order, slot, place):
    picked = jnp.int32(order[0][slot])
    for z in range(1, len(order)):
        picked = jnp.where(place == z, order[z][slot], picked)
    return picked


def spans(requests_ref, count):
    requests = requests_ref[...]
    return [jnp.int32(0)] + [jnp.sum((requests <= r).astype(jnp.int32)) for r in range(count)]


class Meta:
    def __init__(self, ref, requests):
        self.ref, self.requests = ref, requests
        self.adapters = (ref.shape[0] - 2 - requests) // 2
        self.place, self.shard = ref[0], ref[1]

    def adapter(self, r):
        return self.ref[2 + r]

    def rank(self, r):
        return self.ref[2 + self.requests + self.adapter(r)]

    def local_slot(self, r, held):
        return self.ref[2 + self.requests + self.adapters + self.adapter(r)] - self.shard * held


def base_kernel(order, groups, half, held, request_count, *refs):
    slots = [slot for group in groups for slot in group]
    places = [(g, i) for g, group in enumerate(groups) for i in range(len(group))]
    count = len(slots)
    meta, refs = Meta(refs[0], request_count), refs[1:]
    if held:
        requests_ref, factor, refs = refs[0], refs[1], refs[2:]
    hidden, matrix, refs = refs[0], refs[1], refs[2:]
    outs, refs = refs[: len(groups)], refs[len(groups) :]
    (rows, right, sums, sems), refs = refs[:4], refs[4:]
    steps, _, tile = rows.shape
    columns = outs[0].shape[1]
    block = rows.shape[1] // count
    first_rows = [pl.multiple_of(block_at(order, slot, meta.place) * block, block) for slot in slots]

    def depth_of(k):
        return pl.ds(pl.multiple_of(k * tile, tile), tile)

    def copies(k):
        moves = [
            (hidden.at[pl.ds(first_rows[i], block), depth_of(k)], rows.at[k, pl.ds(i * block, block), :])
            for i in range(count)
        ]
        moves.append((matrix.at[depth_of(k), pl.ds(half * columns, columns)], right.at[k]))
        return [pltpu.make_async_copy(a, b, sems.at[k, i]) for i, (a, b) in enumerate(moves)]

    if held:
        factors, inputs, factor_sems = refs
        width = factor.shape[2]

        def factor_copies(k, pair):
            return [
                pltpu.make_async_copy(
                    factor.at[2 * pair + i, depth_of(k), :],
                    factors.at[pair, k, :, pl.ds(i * width, width)],
                    factor_sems.at[k, 2 * pair + i],
                )
                for i in range(2)
            ]

    def start(k):
        for copy in copies(k):
            copy.start()

    def start_factors(k, pairs):
        for pair, used in enumerate(pairs):

            @pl.when(used)
            def _(pair=pair):
                for copy in factor_copies(k, pair):
                    copy.start()

    for k in range(min(AHEAD, steps)):
        start(k)
    used, blocks_using = [], []
    if held:
        bounds = spans(requests_ref, request_count)
        local = [meta.local_slot(r, held) for r in range(request_count)]
        for pair in range(held // 2):
            used_by = []
            for first in first_rows:
                wanted = jnp.bool_(False)
                for r, slot in enumerate(local):
                    here = jnp.maximum(bounds[r], first) < jnp.minimum(bounds[r + 1], first + block)
                    wanted = wanted | (here & (slot // 2 == pair) & (slot >= 0))
                used_by.append(wanted)
            blocks_using.append(used_by)
            used.append(functools.reduce(jnp.logical_or, used_by))
        for k in range(min(AHEAD, steps)):
            start_factors(k, used)
        inputs[...] = jnp.zeros_like(inputs)
    sums[...] = jnp.zeros_like(sums)

    def step(k, _):
        @pl.when(k + AHEAD < steps)
        def _():
            start(k + AHEAD)
            start_factors(k + AHEAD, used)

        for copy in copies(k):
            copy.wait()
        sums[...] += jnp.dot(rows[k], right[k], preferred_element_type=jnp.float32)
        for pair, wanted in enumerate(used):

            @pl.when(wanted)
            def _(pair=pair):
                for copy in factor_copies(k, pair):
                    copy.wait()

            for i, wanted_here in enumerate(blocks_using[pair]):

                @pl.when(wanted_here)
                def _(pair=pair, own=pl.ds(i * block, block)):
                    inputs[pair, own, :] += jnp.dot(
                        rows[k, own, :], factors[pair, k], preferred_element_type=jnp.float32
                    )

        return 0

    lax.fori_loop(0, steps, step, 0)
    piece = outs[0].shape[0] // len(groups[0])
    for i, (group, position) in enumerate(places):
        own = pl.ds(i * block, block)
        out, top = outs[group], position * piece
        out[top : top + block, :] = sums[own, :].astype(jnp.bfloat16)
        if held:
            row = lax.broadcasted_iota(jnp.int32, (block, width), 0) + first_rows[i]
            column = lax.broadcasted_iota(jnp.int32, (block, width), 1)
            total = jnp.zeros((block, width), jnp.float32)
            for r, slot in enumerate(local):
                last = jnp.where((slot >= 0) & (slot < held), bounds[r + 1], 0)
                keep = (row >= bounds[r]) & (row < last) & (column < meta.rank(r))
                slot = jnp.clip(slot, 0, held - 1)
                lanes = pl.ds(pl.multiple_of(slot % 2 * width, width), width)
                total = jnp.where(keep, inputs[slot // 2, own, lanes], total)
            total = total.astype(jnp.bfloat16)
            size = block * width // columns
            for j in range(columns // width):
                lanes = slice(j * width, (j + 1) * width)
                out[top + block : top + block + size, lanes] = total[j * size : (j + 1) * size, :]


def base_terms(meta, requests, request_count, hidden, matrix, factor, groups, half, n, grant):
    tokens, depth = hidden.shape
    block, columns = tokens // n, matrix.shape[1] // 2
    tile = first_divisor(depth, (1024, 512, 256, 128))
    steps = depth // tile
    count = sum(len(group) for group in groups)
    smem = pl.BlockSpec(memory_space=pltpu.SMEM)
    vmem = pl.BlockSpec(memory_space=pltpu.VMEM)
    hbm = pl.BlockSpec(memory_space=pltpu.HBM)
    held, out_rows = 0, block
    operands, in_specs = [meta], [smem]
    scratch = [
        pltpu.VMEM((steps, count * block, tile), jnp.bfloat16),
        pltpu.VMEM((steps, tile, columns), jnp.bfloat16),
        pltpu.VMEM((count * block, columns), jnp.float32),
        pltpu.SemaphoreType.DMA((steps, count + 1)),
    ]
    if factor is not None:
        held, _, width = factor.shape
        out_rows += block * width // columns
        operands, in_specs = [meta, requests, factor], [smem, vmem, hbm]
        scratch += [
            pltpu.VMEM((held // 2, steps, tile, 2 * width), jnp.bfloat16),
            pltpu.VMEM((held // 2, count * block, 2 * width), jnp.float32),
            pltpu.SemaphoreType.DMA((steps, held)),
        ]
    return pl.pallas_call(
        lambda *refs: base_kernel(line_order(n), groups, half, held, request_count, *refs),
        out_shape=[jax.ShapeDtypeStruct((len(group) * out_rows, columns), jnp.bfloat16) for group in groups],
        in_specs=in_specs + [hbm, hbm],
        out_specs=[vmem] * len(groups),
        scratch_shapes=scratch,
        compiler_params=params(grant),
        cost_estimate=small_cost(),
        name="base_terms",
    )(*operands, hidden, matrix)


def select_rows_kernel(request_count, meta_ref, factor, kept, sent):
    meta = Meta(meta_ref, request_count)
    held, rank_rows, _ = factor.shape
    width = factor.shape[2] // (2 * PAIRS)
    side = meta.shard % 2
    for r in range(request_count):
        slot = meta.local_slot(r, held)
        owned = (slot >= 0) & (slot < held)
        slot = jnp.clip(slot, 0, held - 1)
        for out, core in ((kept, side), (sent, 1 - side)):
            for i in range(PAIRS):
                for c in range(2):
                    first = (2 * i + core) * width + c * (width // 2)
                    rows = factor[slot, :, pl.ds(pl.multiple_of(first, LANES), width // 2)]
                    top = (c * request_count + r) * rank_rows
                    out[i, top : top + rank_rows, :] = jnp.where(owned, rows, jnp.zeros_like(rows))


def select_rows(meta, request_count, factor):
    _, rank_rows, model_width = factor.shape
    smem = pl.BlockSpec(memory_space=pltpu.SMEM)
    vmem = pl.BlockSpec(memory_space=pltpu.VMEM)
    shape = (PAIRS, 2 * request_count * rank_rows, model_width // (4 * PAIRS))
    out = jax.ShapeDtypeStruct(shape, factor.dtype)
    return pl.pallas_call(
        lambda *refs: select_rows_kernel(request_count, *refs),
        out_shape=[out, out],
        in_specs=[smem, vmem],
        out_specs=[vmem, vmem],
        compiler_params=params(16),
        cost_estimate=small_cost(),
        name="select_rows",
    )(meta, factor)


def expanded_inputs(meta, requests_ref, lora_ref):
    block, width = lora_ref.shape
    row = lax.broadcasted_iota(jnp.int32, (block, width), 0) + meta.place * block
    lora = lora_ref[...].astype(jnp.float32)
    bounds = spans(requests_ref, meta.requests)
    parts = []
    for r in range(meta.requests):
        scale = 0.25 * width / meta.rank(r).astype(jnp.float32)
        keep = (row >= bounds[r]) & (row < bounds[r + 1])
        parts.append(jnp.where(keep, lora * scale, 0.0).astype(jnp.bfloat16))
    return jnp.concatenate(parts, axis=1)


def finish_kernel(items, added, requests, rank_rows, n, *refs):
    meta_ref, requests_ref, lora_ref, refs = refs[0], refs[1], refs[2], refs[3:]
    arrays, out, rows = refs[:-2], refs[-2], refs[-1]
    meta = Meta(meta_ref, requests)
    rank = n * rank_rows
    half = out.shape[1] // 2
    for index, top, targets in items:
        for place, k in targets:

            @pl.when(meta.place == place)
            def _(piece=arrays[index], top=top, k=k):
                for r in range(requests):
                    first = r * rank + k * rank_rows
                    for c in range(2):
                        start = top + (c * requests + r) * rank_rows
                        rows[first : first + rank_rows, c * half : (c + 1) * half] = piece[start : start + rank_rows, :]

    expanded = expanded_inputs(meta, requests_ref, lora_ref)
    block = lora_ref.shape[0]
    for c in range(2):
        columns = slice(c * half, (c + 1) * half)
        total = jnp.dot(expanded, rows[:, columns], preferred_element_type=jnp.float32)
        for index, top, which in added:
            if which == c:
                total += arrays[index][top : top + block, :].astype(jnp.float32)
        out[:, columns] = total.astype(out.dtype)


def finish(meta, requests, lora, arrays, items, added, request_count, rank_rows, n):
    smem = pl.BlockSpec(memory_space=pltpu.SMEM)
    vmem = pl.BlockSpec(memory_space=pltpu.VMEM)
    width = 2 * arrays[0].shape[1]
    return pl.pallas_call(
        lambda *refs: finish_kernel(items, added, request_count, rank_rows, n, *refs),
        out_shape=jax.ShapeDtypeStruct((lora.shape[0], width), jnp.bfloat16),
        in_specs=[smem] + [vmem] * (2 + len(arrays)),
        out_specs=vmem,
        scratch_shapes=[pltpu.VMEM((request_count * n * rank_rows, width), jnp.bfloat16)],
        compiler_params=params(20),
        cost_estimate=small_cost(),
        name="finish",
    )(meta, requests, lora, *arrays)


def join_kernel(count, term_top, came_top, under_top, term, came, *refs):
    out = refs[-1]
    total = term[term_top : term_top + count, :].astype(jnp.float32)
    total += came[came_top : came_top + count, :].astype(jnp.float32)
    out[:count, :] = total.astype(out.dtype)
    if len(refs) > 1:
        under = refs[0]
        out[count:, :] = under[under_top : under_top + out.shape[0] - count, :]


def join(token, count, term, term_top, came, came_top, under=None, under_top=0, under_count=0):
    arrays = [term, came] + ([] if under is None else [under])
    arrays = lax.optimization_barrier((arrays, token))[0]
    vmem = pl.BlockSpec(memory_space=pltpu.VMEM)
    return pl.pallas_call(
        lambda *refs: join_kernel(count, term_top, came_top, under_top, *refs),
        out_shape=jax.ShapeDtypeStruct((count + under_count, term.shape[1]), term.dtype),
        in_specs=[vmem] * len(arrays),
        out_specs=vmem,
        compiler_params=params(12),
        cost_estimate=small_cost(),
        name="join",
    )(*arrays)


def add_last_kernel(total, up, down, out):
    half = up.shape[1]
    out[:, :half] = total[:, :half]
    last = total[:, half:].astype(jnp.float32) + up[...].astype(jnp.float32) + down[...].astype(jnp.float32)
    out[:, half:] = last.astype(out.dtype)


def add_last(total, up, down):
    vmem = pl.BlockSpec(memory_space=pltpu.VMEM)
    return pl.pallas_call(
        add_last_kernel,
        out_shape=jax.ShapeDtypeStruct(total.shape, total.dtype),
        in_specs=[vmem] * 3,
        out_specs=vmem,
        compiler_params=params(12),
        cost_estimate=small_cost(),
        name="add_last",
    )(total, up, down)


def swap(x, axis, bit):
    return lax.ppermute(x, axis, [(i, i ^ bit) for i in range(lax.axis_size(axis))])


def bits_of(size):
    return [1 << i for i in range(size.bit_length() - 1)]


def along_edge(x, edge):
    n = lax.axis_size("tensor")
    return lax.ppermute(x, "tensor", [(edge, edge + 1), (n - 1 - edge, n - 2 - edge)])


def on_line(hidden, matrix, input_factor, output_factor, requests, token, request_count, n):
    shard = lax.axis_index("store")
    block = hidden.shape[0] // n
    width = input_factor.shape[2]
    rank_rows = output_factor.shape[1]
    piece = block + block * width // (matrix.shape[1] // 2)
    bundle = 2 * request_count * rank_rows

    def base(token, groups, half, grant):
        factor = input_factor if half == 0 else None
        return base_terms(token, requests, request_count, hidden, matrix, factor, groups, half, n, grant)

    def send(x, edge, token):
        return along_edge(after(x, token), edge)

    kept, sent = select_rows(token, request_count, output_factor)
    token = after(token, kept, sent)
    swapped = swap(sent, "store", 1)
    (s00,) = base(token, [[0]], 0, 58)
    token = after(token, s00, swapped)
    e0_1 = along_edge(s00, 0)
    side = shard // 2 % 2
    kept, swapped, _ = lax.optimization_barrier((kept, swapped, token))
    outgoing = kept[1 - side] + swapped[1 - side]
    rows = kept[side] + swapped[side]
    token = after(token, outgoing, rows)
    swapped = swap(outgoing, "store", 2)
    (s01_s11,) = base(token, [[0, 1]], 1, 50)

    token = after(token, s01_s11)
    e0_2 = send(s01_s11, 0, token)
    token, swapped = lax.optimization_barrier((token, swapped))
    rows = rows + swapped
    token = after(token, rows)
    near = lax.ppermute(rows, "tensor", [(0, 1), (n - 1, n - 2), (1, 0), (n - 2, n - 1)])
    b10 = join(token, piece, s00, 0, e0_1, 0, rows, 0, bundle)
    token = after(token, b10)
    e1_2 = along_edge(b10, 1)
    s10_s20, s30 = base(token, [[1, 2], [3]], 0, 42)

    token = after(token, s10_s20)
    e0_3 = send(s10_s20, 0, token)
    token = after(token, e0_2, near, e1_2)
    b11 = join(token, block, s01_s11, 0, e0_2, 0, near, 0, bundle)
    token = after(token, b11)
    e1_3 = along_edge(b11, 1)
    c20 = join(token, piece, s10_s20, piece, e1_2, 0, e1_2, piece, bundle)
    token = after(token, c20)
    e2_3 = along_edge(c20, 2)
    s21, s31 = base(token, [[2], [3]], 1, 50)

    token = after(token, s21)
    e0_4 = send(s21, 0, token)
    token = after(token, e0_3, e1_3, e2_3)
    b20 = join(token, piece, s10_s20, 0, e0_3, 0)
    token = after(token, b20)
    e1_4 = along_edge(b20, 1)
    c21 = join(token, block, s21, 0, e1_3, 0, e1_3, block, bundle)
    token = after(token, c21)
    e2_4 = along_edge(c21, 2)
    b21 = join(token, block, s01_s11, block, e0_2, block)
    token = after(token, b21)
    e1_5 = along_edge(b21, 1)

    lora = s30[block:].astype(jnp.float32) + e0_3[piece + block :].astype(jnp.float32)
    lora += e1_4[block:].astype(jnp.float32) + e2_3[block:piece].astype(jnp.float32)
    lora = lora.astype(jnp.bfloat16).reshape(piece - block, -1, width).swapaxes(0, 1).reshape(block, width)
    lora = lora + swap(lora, "store", 1)
    lora = lora + swap(lora, "store", 2)
    arrays = [s30, s31, rows, near, e1_2, e1_3, e2_3, e2_4, e0_3, e1_4]
    items = [
        (2, 0, [(z, z) for z in range(n)]),
        (3, 0, [(0, 1), (1, 0), (2, 3), (3, 2)]),
        (4, piece, [(1, 2), (2, 1)]),
        (5, block, [(1, 3), (2, 0)]),
        (6, piece, [(0, 2), (3, 1)]),
        (7, block, [(0, 3), (3, 0)]),
    ]
    added = [(0, 0, 0), (8, piece, 0), (9, 0, 0), (6, 0, 0), (1, 0, 1), (7, 0, 1)]
    out = finish(token, requests, lora, arrays, items, added, request_count, rank_rows, n)
    return add_last(out, e0_4, e1_5)


def anywhere(hidden, matrix, input_factor, output_factor, token_requests, meta):
    request_adapters, ranks, slots = meta
    held = input_factor.shape[0]
    width = input_factor.shape[2]
    rank, slot = ranks[request_adapters], slots[request_adapters]
    owned = slot // held == lax.axis_index("store")
    chosen = token_requests[:, None] == jnp.arange(request_adapters.shape[0])[None, :]
    lora = jnp.zeros((hidden.shape[0], width), jnp.float32)
    for r in range(request_adapters.shape[0]):
        product = jnp.dot(hidden, input_factor[slot[r] % held], preferred_element_type=jnp.float32)
        keep = (chosen[:, r] & owned[r])[:, None] & (jnp.arange(width) < rank[r])[None, :]
        lora = jnp.where(keep, product, lora)
    lora = lax.psum_scatter(lora.astype(jnp.bfloat16), "tensor", scatter_dimension=1, tiled=True)
    lora = lax.psum(lora, "store").astype(jnp.float32)
    rows = jnp.where(owned[:, None, None], output_factor[slot % held], jnp.zeros((), output_factor.dtype))
    rows = lax.psum_scatter(rows, "store", scatter_dimension=2, tiled=True)
    weights = jnp.where(chosen, 0.25 * width / rank.astype(jnp.float32)[None, :], 0.0)
    expanded = (weights[:, :, None] * lora[:, None, :]).reshape(hidden.shape[0], -1).astype(jnp.bfloat16)
    term = jnp.dot(hidden, matrix, preferred_element_type=jnp.float32)
    term += jnp.dot(expanded, rows.reshape(-1, rows.shape[2]), preferred_element_type=jnp.float32)
    return lax.psum_scatter(term.astype(jnp.bfloat16), "tensor", scatter_dimension=0, tiled=True)


def per_device(
    hidden_activations,
    down_matrix,
    adapter_input_factor,
    adapter_output_factor,
    token_requests,
    request_adapters,
    adapter_ranks,
    adapter_store_slot,
):
    n = lax.axis_size("tensor")
    meta = (request_adapters, adapter_ranks, adapter_store_slot)
    arrays = (hidden_activations, down_matrix, adapter_input_factor, adapter_output_factor)
    if n == LINE and lax.axis_size("store") == 2 * PAIRS and adapter_input_factor.shape[0] % 2 == 0:
        place = jnp.stack([lax.axis_index("tensor"), lax.axis_index("store")]).astype(jnp.int32)
        token = jnp.concatenate([place, *meta])
        return on_line(*arrays, token_requests.reshape(-1, LANES), token, request_adapters.shape[0], n)
    return anywhere(*arrays, token_requests, meta)


def solution(mesh):
    in_specs = (
        P("groups", "tensor"),
        P("tensor", "store"),
        P(("groups", "store"), "tensor", None),
        P(("groups", "store"), "tensor", None),
        P("groups"),
        P("groups"),
        P("groups"),
        P("groups"),
    )
    out_specs = P(("groups", "tensor"), "store")
    return jax.shard_map(
        per_device, mesh=mesh, in_specs=in_specs, out_specs=out_specs, check_vma=False
    )
```

profile of v0, /device:TPU:0, one launch (start us, length us, event | category | flops | bytes accessed | tf_op | source)
XLA Modules:
  0.0 134.2 jit_solution(5914214869343089694)
XLA Ops:
  0.0 0.8 concatenate.3.refs_0_
  0.8 1.6 %copy-done.3 = bf16[4,32,8192]{2,1,0:T(8,128)(2,1)S(1)} copy-done((bf16[4,32,8192]{2,1,0:T(8,128)(2,1)S(1)}, bf16[4,32,8192]{2,1,0:T(8,128)(2,1)}, u32[]{:S(2)}) %copy-start.3) | copy-done | bytes 2097176
  2.4 0.8 select_rows.1
  3.2 0.5 collective-permute-start
  3.7 9.3 %base_terms.4.refs_0_ = bf16[288,1024]{1,0:T(8,128)(2,1)} custom-call(s32[38]{0:T(128)} %copy-done.7, s32[8,128]{1,0:T(8,128)} %bitcast.16, bf16[4,7168,128]{2,1,0:T(8,128)(2,1)} %refs_2_.6, bf16[1024,7168]{1,0:T(8,128)(2,1)} %refs_1_.5, bf16[7168,2048]{1,0:T(8,128)(2,1)} %refs_2_.7), custom_call_target="tpu_custom_call" | custom-call | flops 1000000 | bytes 100000 | tf_op jit(solution)/shard_map/base_terms/pallas_call | solution.py:221
  13.0 5.3 %collective-permute-start.2 = (bf16[288,1024]{1,0:T(8,128)(2,1)}, bf16[288,1024]{1,0:T(8,128)(2,1)}, u32[]{:S(2)}, u32[]{:S(2)}) collective-permute-start(bf16[288,1024]{1,0:T(8,128)(2,1)} %base_terms.4.refs_0_), channel_id=1, source_target_pairs={{0,4},{12,8},{1,5},{13,9},{2,6},{14,10},{3,7},{15,11},{16,20},{28,... | collective-permute-start | bytes 1769480 | tf_op jit(solution)/shard_map/ppermute | solution.py:380
  18.4 1.6 %collective-permute-start.1 = (bf16[256,1024]{1,0:T(8,128)(2,1)S(1)}, bf16[256,1024]{1,0:T(8,128)(2,1)S(1)}, u32[]{:S(2)}, u32[]{:S(2)}) collective-permute-start(bf16[256,1024]{1,0:T(8,128)(2,1)S(1)} %get-tuple-element.94), channel_id=1, source_target_pairs={{0,2},{1,3},{2,0},{3,1},{4,6},{5,7},{6,4},{7,5},{8,10},{9,11},{10,... | collective-permute-start | bytes 1572872 | tf_op jit(solution)/shard_map/ppermute | solution.py:371
  20.0 11.8 %base_terms.5.refs_0_ = bf16[512,1024]{1,0:T(8,128)(2,1)S(1)} custom-call(s32[38]{0:T(128)S(1)} %copy-done.8, bf16[1024,7168]{1,0:T(8,128)(2,1)} %refs_1_.5, bf16[7168,2048]{1,0:T(8,128)(2,1)} %refs_2_.7), custom_call_target="tpu_custom_call" | custom-call | flops 1000000 | bytes 100000 | tf_op jit(solution)/shard_map/base_terms/pallas_call | solution.py:221
  32.1 0.8 copy-done
  32.9 1.2 join.6
  34.1 0.7 collective-permute-start.5
  34.9 8.0 %collective-permute-start.3 = (bf16[512,1024]{1,0:T(8,128)(2,1)S(1)}, bf16[512,1024]{1,0:T(8,128)(2,1)S(1)}, u32[]{:S(2)}, u32[]{:S(2)}) collective-permute-start(bf16[512,1024]{1,0:T(8,128)(2,1)S(1)} %base_terms.5.refs_0_), channel_id=1, source_target_pairs={{0,4},{12,8},{1,5},{13,9},{2,6},{14,10},{3,7},{15,11},{16,20},{28,... | collective-permute-start | bytes 3145736 | tf_op jit(solution)/shard_map/ppermute | solution.py:380
  43.0 21.0 %base_terms.6 = (bf16[576,1024]{1,0:T(8,128)(2,1)S(1)}, bf16[288,1024]{1,0:T(8,128)(2,1)S(1)}) custom-call(s32[38]{0:T(128)S(1)} %copy-done.8, s32[8,128]{1,0:T(8,128)S(1)} %bitcast.17, bf16[4,7168,128]{2,1,0:T(8,128)(2,1)S(1)} %bitcast.15, bf16[1024,7168]{1,0:T(8,128)(2,1)} %refs_1_.5, bf16[7168,2048]{1,0:T(8,128)(2,1)} %refs_2_.7), custom_call_target="tpu_custom_call" | custom-call | flops 1000000 | bytes 100000 | tf_op jit(solution)/shard_map/base_terms/pallas_call | solution.py:221
  64.0 0.8 copy-done.4
  64.8 3.9 %collective-permute-start.6 = (bf16[576,1024]{1,0:T(8,128)(2,1)S(1)}, bf16[576,1024]{1,0:T(8,128)(2,1)S(1)}, u32[]{:S(2)}, u32[]{:S(2)}) collective-permute-start(bf16[576,1024]{1,0:T(8,128)(2,1)S(1)} %get-tuple-element.80.refs_0_), channel_id=1, source_target_pairs={{0,4},{12,8},{1,5},{13,9},{2,6},{14,10},{3,7},{15,11},{16,20},{28,... | collective-permute-start | bytes 3538952 | tf_op jit(solution)/shard_map/ppermute | solution.py:380
  68.8 8.9 %collective-permute-done.4.refs_2_.refs_6_ = bf16[256,1024]{1,0:T(8,128)(2,1)S(1)} collective-permute-done((bf16[256,1024]{1,0:T(8,128)(2,1)S(1)}, bf16[256,1024]{1,0:T(8,128)(2,1)S(1)}, u32[]{:S(2)}, u32[]{:S(2)}) %collective-permute-start.4) | collective-permute-done | bytes 524320 | tf_op jit(solution)/shard_map/ppermute | solution.py:417
  77.8 0.7 copy-done.1
  78.6 1.3 collective-permute-start.8
  79.9 0.7 collective-permute-start.7
  80.7 11.6 %base_terms.7 = (bf16[256,1024]{1,0:T(8,128)(2,1)S(1)}, bf16[256,1024]{1,0:T(8,128)(2,1)S(1)}) custom-call(s32[38]{0:T(128)S(1)} %copy-done.8, bf16[1024,7168]{1,0:T(8,128)(2,1)} %refs_1_.5, bf16[7168,2048]{1,0:T(8,128)(2,1)} %refs_2_.7), custom_call_target="tpu_custom_call" | custom-call | flops 1000000 | bytes 100000 | tf_op jit(solution)/shard_map/base_terms/pallas_call | solution.py:221
  92.3 9.0 %collective-permute-done.6.refs_1_.refs_11_ = bf16[576,1024]{1,0:T(8,128)(2,1)S(1)} collective-permute-done((bf16[576,1024]{1,0:T(8,128)(2,1)S(1)}, bf16[576,1024]{1,0:T(8,128)(2,1)S(1)}, u32[]{:S(2)}, u32[]{:S(2)}) %collective-permute-start.6) | collective-permute-done | bytes 1179680 | tf_op jit(solution)/shard_map/ppermute | solution.py:380
  101.3 2.6 %collective-permute-done.8.refs_9_ = bf16[544,1024]{1,0:T(8,128)(2,1)S(1)} collective-permute-done((bf16[544,1024]{1,0:T(8,128)(2,1)S(1)}, bf16[544,1024]{1,0:T(8,128)(2,1)S(1)}, u32[]{:S(2)}, u32[]{:S(2)}) %collective-permute-start.8) | collective-permute-done | bytes 1114144 | tf_op jit(solution)/shard_map/ppermute | solution.py:380
  104.1 0.7 collective-permute-start.9
  105.0 1.4 %collective-permute-start.12 = (bf16[512,1024]{1,0:T(8,128)(2,1)S(1)}, bf16[512,1024]{1,0:T(8,128)(2,1)S(1)}, u32[]{:S(2)}, u32[]{:S(2)}) collective-permute-start(bf16[512,1024]{1,0:T(8,128)(2,1)S(1)} %join.10), channel_id=1, source_target_pairs={{8,12},{4,0},{9,13},{5,1},{10,14},{6,2},{11,15},{7,3},{24,28},{20,... | collective-permute-start | bytes 3145736 | tf_op jit(solution)/shard_map/ppermute | solution.py:380
  106.4 6.8 %collective-permute-start.13 = (bf16[256,1024]{1,0:T(8,128)(2,1)S(1)}, bf16[256,1024]{1,0:T(8,128)(2,1)S(1)}, u32[]{:S(2)}, u32[]{:S(2)}) collective-permute-start(bf16[256,1024]{1,0:T(8,128)(2,1)S(1)} %get-tuple-element.92.refs_0_), channel_id=1, source_target_pairs={{0,4},{12,8},{1,5},{13,9},{2,6},{14,10},{3,7},{15,11},{16,20},{28,... | collective-permute-start | bytes 1572872 | tf_op jit(solution)/shard_map/ppermute | solution.py:380
  113.3 0.7 collective-permute-start.14
  114.2 1.2 collective-permute-done.10
  115.5 1.4 %collective-permute-start.11 = (bf16[256,128]{1,0:T(8,128)(2,1)S(1)}, bf16[256,128]{1,0:T(8,128)(2,1)S(1)}, u32[]{:S(2)}, u32[]{:S(2)}) collective-permute-start(bf16[256,128]{1,0:T(8,128)(2,1)S(1)} %bitcast_add_fusion), channel_id=1, source_target_pairs={{0,2},{1,3},{2,0},{3,1},{4,6},{5,7},{6,4},{7,5},{8,10},{9,11},{10,... | collective-permute-start | bytes 196616 | tf_op jit(solution)/shard_map/ppermute | solution.py:371
  116.9 2.9 %collective-permute-done.11 = bf16[256,128]{1,0:T(8,128)(2,1)S(1)} collective-permute-done((bf16[256,128]{1,0:T(8,128)(2,1)S(1)}, bf16[256,128]{1,0:T(8,128)(2,1)S(1)}, u32[]{:S(2)}, u32[]{:S(2)}) %collective-permute-start.11) | collective-permute-done | bytes 65568 | tf_op jit(solution)/shard_map/ppermute | solution.py:371
  119.8 11.4 %collective-permute-done.12.refs_10_ = bf16[512,1024]{1,0:T(8,128)(2,1)S(1)} collective-permute-done((bf16[512,1024]{1,0:T(8,128)(2,1)S(1)}, bf16[512,1024]{1,0:T(8,128)(2,1)S(1)}, u32[]{:S(2)}, u32[]{:S(2)}) %collective-permute-start.12) | collective-permute-done | bytes 1048608 | tf_op jit(solution)/shard_map/ppermute | solution.py:380
  131.2 1.8 %finish.1.total = bf16[256,2048]{1,0:T(8,128)(2,1)S(1)} custom-call(s32[38]{0:T(128)S(1)} %copy-done.8, s32[8,128]{1,0:T(8,128)S(1)} %bitcast.18, bf16[256,128]{1,0:T(8,128)(2,1)S(1)} %add.56.refs_2_, bf16[288,1024]{1,0:T(8,128)(2,1)S(1)} %copy-done.5, bf16[256,1024]{1,0:T(8,128)(2,1)S(1)} %get-tuple-element.91.refs_4_, ...), custom_call_target="tpu_custom_call" | custom-call | flops 1000000 | bytes 100000 | tf_op jit(solution)/shard_map/finish/pallas_call | solution.py:313
  133.1 1.2 add_last.1
  (42 shorter events, 1.3 us)
Async XLA Ops:
  0.8 1.6 %copy-start.3 = (bf16[4,32,8192]{2,1,0:T(8,128)(2,1)S(1)}, bf16[4,32,8192]{2,1,0:T(8,128)(2,1)}, u32[]{:S(2)}) copy-start(bf16[4,32,8192]{2,1,0:T(8,128)(2,1)} %refs_1_.3) | copy-start | bytes 6291460
  2.4 1.4 %copy-start.7 = (s32[38]{0:T(128)}, s32[38]{0:T(128)S(1)}, u32[]{:S(2)}) copy-start(s32[38]{0:T(128)S(1)} %concatenate.3.refs_0_) | copy-start | bytes 460
  3.2 15.2 %collective-permute-start = (bf16[2,256,1024]{2,1,0:T(8,128)(2,1)S(1)}, bf16[2,256,1024]{2,1,0:T(8,128)(2,1)S(1)}, u32[]{:S(2)}, u32[]{:S(2)}) collective-permute-start(bf16[2,256,1024]{2,1,0:T(8,128)(2,1)S(1)} %get-tuple-element.50), channel_id=1, source_target_pairs={{0,1},{1,0},{2,3},{3,2},{4,5},{5,4},{6,7},{7,6},{8,9},{9,8},{10,11... | collective-permute-start | bytes 3145736 | tf_op jit(solution)/shard_map/ppermute | solution.py:371
  13.0 19.1 %collective-permute-start.2 = (bf16[288,1024]{1,0:T(8,128)(2,1)}, bf16[288,1024]{1,0:T(8,128)(2,1)}, u32[]{:S(2)}, u32[]{:S(2)}) collective-permute-start(bf16[288,1024]{1,0:T(8,128)(2,1)} %base_terms.4.refs_0_), channel_id=1, source_target_pairs={{0,4},{12,8},{1,5},{13,9},{2,6},{14,10},{3,7},{15,11},{16,20},{28,... | collective-permute-start | bytes 1769480 | tf_op jit(solution)/shard_map/ppermute | solution.py:380
  18.3 1.7 %copy-start.8 = (s32[38]{0:T(128)S(1)}, s32[38]{0:T(128)}, u32[]{:S(2)}) copy-start(s32[38]{0:T(128)} %copy-done.7) | copy-start | bytes 460
  18.4 13.4 %collective-permute-start.1 = (bf16[256,1024]{1,0:T(8,128)(2,1)S(1)}, bf16[256,1024]{1,0:T(8,128)(2,1)S(1)}, u32[]{:S(2)}, u32[]{:S(2)}) collective-permute-start(bf16[256,1024]{1,0:T(8,128)(2,1)S(1)} %get-tuple-element.94), channel_id=1, source_target_pairs={{0,2},{1,3},{2,0},{3,1},{4,6},{5,7},{6,4},{7,5},{8,10},{9,11},{10,... | collective-permute-start | bytes 1572872 | tf_op jit(solution)/shard_map/ppermute | solution.py:371
  20.0 23.0 %slice-start = ((s8[7340032]{0:T(1024)(128)(4,1)}), s8[4194304]{0:T(1024)(128)(4,1)S(1)}, s32[]{:S(2)}) async-start(s8[7340032]{0:T(1024)(128)(4,1)} %bitcast.14), calls=%async_computation | async-start | bytes 8388608
  20.0 23.0 %slice-start.1 = ((s8[7340032]{0:T(1024)(128)(4,1)}), s8[3145728]{0:T(1024)(128)(4,1)S(1)}, s32[]{:S(2)}) async-start(s8[7340032]{0:T(1024)(128)(4,1)} %bitcast.14), calls=%async_computation.1 | async-start | bytes 6291456
  31.9 1.1 copy-start
  32.1 10.9 %copy-start.6 = (s32[1024]{0:T(1024)S(1)}, s32[1024]{0:T(1024)}, u32[]{:S(2)}) copy-start(s32[1024]{0:T(1024)} %param.12) | copy-start | bytes 12292
  34.1 43.5 %collective-permute-start.5 = (bf16[544,1024]{1,0:T(8,128)(2,1)S(1)}, bf16[544,1024]{1,0:T(8,128)(2,1)S(1)}, u32[]{:S(2)}, u32[]{:S(2)}) collective-permute-start(bf16[544,1024]{1,0:T(8,128)(2,1)S(1)} %join.6), channel_id=1, source_target_pairs={{4,8},{8,4},{5,9},{9,5},{6,10},{10,6},{7,11},{11,7},{20,24},{24,20... | collective-permute-start | bytes 3342344 | tf_op jit(solution)/shard_map/ppermute | solution.py:380
  34.9 42.8 %collective-permute-start.3 = (bf16[512,1024]{1,0:T(8,128)(2,1)S(1)}, bf16[512,1024]{1,0:T(8,128)(2,1)S(1)}, u32[]{:S(2)}, u32[]{:S(2)}) collective-permute-start(bf16[512,1024]{1,0:T(8,128)(2,1)S(1)} %base_terms.5.refs_0_), channel_id=1, source_target_pairs={{0,4},{12,8},{1,5},{13,9},{2,6},{14,10},{3,7},{15,11},{16,20},{28,... | collective-permute-start | bytes 3145736 | tf_op jit(solution)/shard_map/ppermute | solution.py:380
  42.9 34.8 %collective-permute-start.4 = (bf16[256,1024]{1,0:T(8,128)(2,1)S(1)}, bf16[256,1024]{1,0:T(8,128)(2,1)S(1)}, u32[]{:S(2)}, u32[]{:S(2)}) collective-permute-start(bf16[256,1024]{1,0:T(8,128)(2,1)S(1)} %add.51.refs_2_.refs_5_), channel_id=1, source_target_pairs={{0,4},{12,8},{4,0},{8,12},{1,5},{13,9},{5,1},{9,13},{2,6},{14,10},... | collective-permute-start | bytes 1572872 | tf_op jit(solution)/shard_map/ppermute | solution.py:417
  64.0 0.8 copy-start.4
  64.8 36.5 %collective-permute-start.6 = (bf16[576,1024]{1,0:T(8,128)(2,1)S(1)}, bf16[576,1024]{1,0:T(8,128)(2,1)S(1)}, u32[]{:S(2)}, u32[]{:S(2)}) collective-permute-start(bf16[576,1024]{1,0:T(8,128)(2,1)S(1)} %get-tuple-element.80.refs_0_), channel_id=1, source_target_pairs={{0,4},{12,8},{1,5},{13,9},{2,6},{14,10},{3,7},{15,11},{16,20},{28,... | collective-permute-start | bytes 3538952 | tf_op jit(solution)/shard_map/ppermute | solution.py:380
  77.7 0.8 copy-start.1
  78.6 25.3 %collective-permute-start.8 = (bf16[544,1024]{1,0:T(8,128)(2,1)S(1)}, bf16[544,1024]{1,0:T(8,128)(2,1)S(1)}, u32[]{:S(2)}, u32[]{:S(2)}) collective-permute-start(bf16[544,1024]{1,0:T(8,128)(2,1)S(1)} %join.8), channel_id=1, source_target_pairs={{8,12},{4,0},{9,13},{5,1},{10,14},{6,2},{11,15},{7,3},{24,28},{20,... | collective-permute-start | bytes 3342344 | tf_op jit(solution)/shard_map/ppermute | solution.py:380
  79.9 21.4 %collective-permute-start.7 = (bf16[512,1024]{1,0:T(8,128)(2,1)S(1)}, bf16[512,1024]{1,0:T(8,128)(2,1)S(1)}, u32[]{:S(2)}, u32[]{:S(2)}) collective-permute-start(bf16[512,1024]{1,0:T(8,128)(2,1)S(1)} %join.7), channel_id=1, source_target_pairs={{4,8},{8,4},{5,9},{9,5},{6,10},{10,6},{7,11},{11,7},{20,24},{24,20... | collective-permute-start | bytes 3145736 | tf_op jit(solution)/shard_map/ppermute | solution.py:380
  104.1 10.0 %collective-permute-start.9 = (bf16[288,1024]{1,0:T(8,128)(2,1)S(1)}, bf16[288,1024]{1,0:T(8,128)(2,1)S(1)}, u32[]{:S(2)}, u32[]{:S(2)}) collective-permute-start(bf16[288,1024]{1,0:T(8,128)(2,1)S(1)} %join.9), channel_id=1, source_target_pairs={{4,8},{8,4},{5,9},{9,5},{6,10},{10,6},{7,11},{11,7},{20,24},{24,20... | collective-permute-start | bytes 1769480 | tf_op jit(solution)/shard_map/ppermute | solution.py:380
  104.9 9.1 %copy-start.5 = (bf16[288,1024]{1,0:T(8,128)(2,1)S(1)}, bf16[288,1024]{1,0:T(8,128)(2,1)}, u32[]{:S(2)}) copy-start(bf16[288,1024]{1,0:T(8,128)(2,1)} %copy-done.4) | copy-start | bytes 1769476
  105.0 26.3 %copy-start.2 = (bf16[256,1024]{1,0:T(8,128)(2,1)S(1)}, bf16[256,1024]{1,0:T(8,128)(2,1)}, u32[]{:S(2)}) copy-start(bf16[256,1024]{1,0:T(8,128)(2,1)} %copy-done.1) | copy-start | bytes 1572868
  105.0 26.3 %collective-permute-start.12 = (bf16[512,1024]{1,0:T(8,128)(2,1)S(1)}, bf16[512,1024]{1,0:T(8,128)(2,1)S(1)}, u32[]{:S(2)}, u32[]{:S(2)}) collective-permute-start(bf16[512,1024]{1,0:T(8,128)(2,1)S(1)} %join.10), channel_id=1, source_target_pairs={{8,12},{4,0},{9,13},{5,1},{10,14},{6,2},{11,15},{7,3},{24,28},{20,... | collective-permute-start | bytes 3145736 | tf_op jit(solution)/shard_map/ppermute | solution.py:380
  106.4 26.6 %collective-permute-start.13 = (bf16[256,1024]{1,0:T(8,128)(2,1)S(1)}, bf16[256,1024]{1,0:T(8,128)(2,1)S(1)}, u32[]{:S(2)}, u32[]{:S(2)}) collective-permute-start(bf16[256,1024]{1,0:T(8,128)(2,1)S(1)} %get-tuple-element.92.refs_0_), channel_id=1, source_target_pairs={{0,4},{12,8},{1,5},{13,9},{2,6},{14,10},{3,7},{15,11},{16,20},{28,... | collective-permute-start | bytes 1572872 | tf_op jit(solution)/shard_map/ppermute | solution.py:380
  113.3 19.7 %collective-permute-start.14 = (bf16[256,1024]{1,0:T(8,128)(2,1)S(1)}, bf16[256,1024]{1,0:T(8,128)(2,1)S(1)}, u32[]{:S(2)}, u32[]{:S(2)}) collective-permute-start(bf16[256,1024]{1,0:T(8,128)(2,1)S(1)} %join.11), channel_id=1, source_target_pairs={{4,8},{8,4},{5,9},{9,5},{6,10},{10,6},{7,11},{11,7},{20,24},{24,20... | collective-permute-start | bytes 1572872 | tf_op jit(solution)/shard_map/ppermute | solution.py:380
  114.2 1.3 collective-permute-start.10
  115.5 4.3 %collective-permute-start.11 = (bf16[256,128]{1,0:T(8,128)(2,1)S(1)}, bf16[256,128]{1,0:T(8,128)(2,1)S(1)}, u32[]{:S(2)}, u32[]{:S(2)}) collective-permute-start(bf16[256,128]{1,0:T(8,128)(2,1)S(1)} %bitcast_add_fusion), channel_id=1, source_target_pairs={{0,2},{1,3},{2,0},{3,1},{4,6},{5,7},{6,4},{7,5},{8,10},{9,11},{10,... | collective-permute-start | bytes 196616 | tf_op jit(solution)/shard_map/ppermute | solution.py:371
where the time goes:
time: 135 us; the launch traced here: 134 us
  Pallas kernels  59.5 us (44%)
  waiting for transfers between devices  36.1 us (27%)
  starting transfers between devices  33.3 us (25%)
  local copies, waits for them, and re-layouts  4.71 us (3%)
    pallas_call x4, Pallas kernels, base_terms(): pl.pallas_call(lambda *refs: base_kernel(line_order(n), groups, half, hel...  53.7 us
    ppermute x10, starting transfers between devices, along_edge(): lax.ppermute(x, 'tensor', [(edge, edge + 1), (n - 1 - edge, n - 2 - edge)])  29.7 us
    ppermute x10, waiting for transfers between devices, along_edge(): lax.ppermute(x, 'tensor', [(edge, edge + 1), (n - 1 - edge, n - 2 - edge)])  23.1 us
    ppermute x1, waiting for transfers between devices, on_line(): lax.ppermute(rows, 'tensor', [(0, 1), (n - 1, n - 2), (1, 0), (n - 2, n -...  8.86 us
    ppermute x4, waiting for transfers between devices, swap(): lax.ppermute(x, axis, [(i, i ^ bit) for i in range(lax.axis_size(axis))])  4.14 us
    unnamed x23, local copies, waits for them, and re-layouts  3.94 us
    ppermute x4, starting transfers between devices, swap(): lax.ppermute(x, axis, [(i, i ^ bit) for i in range(lax.axis_size(axis))])  3.58 us
  transfers between devices with their start and end apart: 15, of which 6 were waited for; matrix products, arithmetic and copies ran while one was open for 0% of the time, Pallas kernels for 42%

commit v1 on v0

--- a/solution.py
+++ b/solution.py
@@ -70,7 +70,7 @@
         return self.ref[2 + self.requests + self.adapters + self.adapter(r)] - self.shard * held
 
 
-def base_kernel(order, groups, half, held, request_count, *refs):
+def base_kernel(order, groups, half, held, request_count, piece, *refs):
     slots = [slot for group in groups for slot in group]
     places = [(g, i) for g, group in enumerate(groups) for i in range(len(group))]
     count = len(slots)
@@ -170,7 +170,6 @@
         return 0
 
     lax.fori_loop(0, steps, step, 0)
-    piece = outs[0].shape[0] // len(groups[0])
     for i, (group, position) in enumerate(places):
         own = pl.ds(i * block, block)
         out, top = outs[group], position * piece
@@ -219,7 +218,7 @@
             pltpu.SemaphoreType.DMA((steps, held)),
         ]
     return pl.pallas_call(
-        lambda *refs: base_kernel(line_order(n), groups, half, held, request_count, *refs),
+        lambda *refs: base_kernel(line_order(n), groups, half, held, request_count, out_rows, *refs),
         out_shape=[jax.ShapeDtypeStruct((len(group) * out_rows, columns), jnp.bfloat16) for group in groups],
         in_specs=in_specs + [hbm, hbm],
         out_specs=[vmem] * len(groups),
@@ -407,10 +406,10 @@
     rows = kept[side] + swapped[side]
     token = after(token, outgoing, rows)
     swapped = swap(outgoing, "store", 2)
-    (s01_s11,) = base(token, [[0, 1]], 1, 50)
-
-    token = after(token, s01_s11)
-    e0_2 = send(s01_s11, 0, token)
+    (s01,) = base(token, [[0]], 1, 50)
+
+    token = after(token, s01)
+    e0_2 = send(s01, 0, token)
     token, swapped = lax.optimization_barrier((token, swapped))
     rows = rows + swapped
     token = after(token, rows)
@@ -422,28 +421,31 @@
 
     token = after(token, s10_s20)
     e0_3 = send(s10_s20, 0, token)
-    token = after(token, e0_2, near, e1_2)
-    b11 = join(token, block, s01_s11, 0, e0_2, 0, near, 0, bundle)
+    token = after(token, e0_2, near)
+    b11 = join(token, block, s01, 0, e0_2, 0, near, 0, bundle)
     token = after(token, b11)
     e1_3 = along_edge(b11, 1)
     c20 = join(token, piece, s10_s20, piece, e1_2, 0, e1_2, piece, bundle)
     token = after(token, c20)
     e2_3 = along_edge(c20, 2)
-    s21, s31 = base(token, [[2], [3]], 1, 50)
-
-    token = after(token, s21)
-    e0_4 = send(s21, 0, token)
-    token = after(token, e0_3, e1_3, e2_3)
+    s11, s21, s31 = base(token, [[1], [2], [3]], 1, 50)
+
+    token = after(token, s11, e0_3)
+    e0_4 = send(s11, 0, token)
     b20 = join(token, piece, s10_s20, 0, e0_3, 0)
     token = after(token, b20)
     e1_4 = along_edge(b20, 1)
+    token = after(token, e1_3, e2_3)
     c21 = join(token, block, s21, 0, e1_3, 0, e1_3, block, bundle)
     token = after(token, c21)
     e2_4 = along_edge(c21, 2)
-    b21 = join(token, block, s01_s11, block, e0_2, block)
+    e0_5 = send(s21, 0, token)
+
+    token, e0_4 = lax.optimization_barrier((token, e0_4))
+    b21 = join(token, block, s11, 0, e0_4, 0)
     token = after(token, b21)
     e1_5 = along_edge(b21, 1)
-
+    e1_4 = lax.optimization_barrier((e1_4, token))[0]
     lora = s30[block:].astype(jnp.float32) + e0_3[piece + block :].astype(jnp.float32)
     lora += e1_4[block:].astype(jnp.float32) + e2_3[block:piece].astype(jnp.float32)
     lora = lora.astype(jnp.bfloat16).reshape(piece - block, -1, width).swapaxes(0, 1).reshape(block, width)
@@ -460,7 +462,7 @@
     ]
     added = [(0, 0, 0), (8, piece, 0), (9, 0, 0), (6, 0, 0), (1, 0, 1), (7, 0, 1)]
     out = finish(token, requests, lora, arrays, items, added, request_count, rank_rows, n)
-    return add_last(out, e0_4, e1_5)
+    return add_last(out, e0_5, e1_5)
 
 
 def anywhere(hidden, matrix, input_factor, output_factor, token_requests, meta):

time: 135 us -> 125 us (0.926)
  waiting for transfers between devices: 36.1 us -> 27 us
  starting transfers between devices: 33.3 us -> 37.7 us
  Pallas kernels: 59.5 us -> 55.4 us
  local copies, waits for them, and re-layouts: 4.71 us -> 2.4 us
    ppermute x10 -> x11, waiting for transfers between devices: 23.1 us -> 15.9 us  [along_edge(): lax.ppermute(x, 'tensor', [(edge, edge + 1), (n - 1 - edge, n - 2 - edge)])]
    ppermute x1, waiting for transfers between devices: 8.86 us -> 2.9 us  [on_line(): lax.ppermute(rows, 'tensor', [(0, 1), (n - 1, n - 2), (1, 0), (n - 2, n -...]
    ppermute x4, waiting for transfers between devices: 4.14 us -> 8.17 us  [swap(): lax.ppermute(x, axis, [(i, i ^ bit) for i in range(lax.axis_size(axis))])]
    pallas_call x4, Pallas kernels: 53.7 us -> 49.9 us  [base_terms(): pl.pallas_call(lambda *refs: base_kernel(line_order(n), groups, half, hel...]
    ppermute x4, starting transfers between devices: 3.58 us -> 6.04 us  [swap(): lax.ppermute(x, axis, [(i, i ^ bit) for i in range(lax.axis_size(axis))])]
    unnamed x23 -> x15, local copies, waits for them, and re-layouts: 3.94 us -> 1.63 us
    ppermute x10 -> x11, starting transfers between devices: 29.7 us -> 31.6 us  [along_edge(): lax.ppermute(x, 'tensor', [(edge, edge + 1), (n - 1 - edge, n - 2 - edge)])]
  transfers between devices with their start and end apart: 15 -> 16, of which waited for: 6 -> 7; matrix products, arithmetic and copies ran while one was open for 0% -> 1% of each run, Pallas kernels for 42% -> 42%
where the time goes in v1:
time: 125 us; the launch traced here: 124 us
  Pallas kernels  55.4 us (44%)
  starting transfers between devices  37.7 us (30%)
  waiting for transfers between devices  27 us (22%)
  local copies, waits for them, and re-layouts  2.4 us (2%)
  other arithmetic  1.58 us (1%)
    pallas_call x4, Pallas kernels, base_terms(): pl.pallas_call(lambda *refs: base_kernel(line_order(n), groups, half, hel...  49.9 us
    ppermute x11, starting transfers between devices, along_edge(): lax.ppermute(x, 'tensor', [(edge, edge + 1), (n - 1 - edge, n - 2 - edge)])  31.6 us
    ppermute x11, waiting for transfers between devices, along_edge(): lax.ppermute(x, 'tensor', [(edge, edge + 1), (n - 1 - edge, n - 2 - edge)])  15.9 us
    ppermute x4, waiting for transfers between devices, swap(): lax.ppermute(x, axis, [(i, i ^ bit) for i in range(lax.axis_size(axis))])  8.17 us
    ppermute x4, starting transfers between devices, swap(): lax.ppermute(x, axis, [(i, i ^ bit) for i in range(lax.axis_size(axis))])  6.04 us
    ppermute x1, waiting for transfers between devices, on_line(): lax.ppermute(rows, 'tensor', [(0, 1), (n - 1, n - 2), (1, 0), (n - 2, n -...  2.9 us
  transfers between devices with their start and end apart: 16, of which 7 were waited for; matrix products, arithmetic and copies ran while one was open for 1% of the time, Pallas kernels for 42%

profile of v1, /device:TPU:0, one launch (start us, length us, event | category | flops | bytes accessed | tf_op | source)
XLA Modules:
  0.0 124.5 jit_solution(14717762269027349248)
XLA Ops:
  0.0 0.8 concatenate.3.refs_0_
  0.8 1.6 %copy-done.1 = bf16[4,32,8192]{2,1,0:T(8,128)(2,1)S(1)} copy-done((bf16[4,32,8192]{2,1,0:T(8,128)(2,1)S(1)}, bf16[4,32,8192]{2,1,0:T(8,128)(2,1)}, u32[]{:S(2)}) %copy-start.1) | copy-done | bytes 2097176
  2.4 1.7 %select_rows.1 = (bf16[2,256,1024]{2,1,0:T(8,128)(2,1)S(1)}, bf16[2,256,1024]{2,1,0:T(8,128)(2,1)}) custom-call(s32[38]{0:T(128)S(1)} %concatenate.3.refs_0_, bf16[4,32,8192]{2,1,0:T(8,128)(2,1)S(1)} %copy-done.1), custom_call_target="tpu_custom_call" | custom-call | flops 1000000 | bytes 100000 | tf_op jit(solution)/shard_map/select_rows/pallas_call | solution.py:256
  4.1 0.5 collective-permute-start
  4.5 9.3 %base_terms.4.refs_0_ = bf16[288,1024]{1,0:T(8,128)(2,1)} custom-call(s32[38]{0:T(128)} %copy-done.3, s32[8,128]{1,0:T(8,128)} %bitcast.16, bf16[4,7168,128]{2,1,0:T(8,128)(2,1)} %refs_2_.6, bf16[1024,7168]{1,0:T(8,128)(2,1)} %refs_1_.5, bf16[7168,2048]{1,0:T(8,128)(2,1)} %refs_2_.7), custom_call_target="tpu_custom_call" | custom-call | flops 1000000 | bytes 100000 | tf_op jit(solution)/shard_map/base_terms/pallas_call | solution.py:220
  13.9 4.5 %collective-permute-start.2 = (bf16[288,1024]{1,0:T(8,128)(2,1)}, bf16[288,1024]{1,0:T(8,128)(2,1)S(1)}, u32[]{:S(2)}, u32[]{:S(2)}) collective-permute-start(bf16[288,1024]{1,0:T(8,128)(2,1)} %base_terms.4.refs_0_), channel_id=1, source_target_pairs={{0,4},{12,8},{1,5},{13,9},{2,6},{14,10},{3,7},{15,11},{16,20},{28,... | collective-permute-start | bytes 1769480 | tf_op jit(solution)/shard_map/ppermute | solution.py:379
  18.4 1.3 %add_bitcast_fusion = (bf16[256,1024]{1,0:T(8,128)(2,1)S(1)}, bf16[256,1024]{1,0:T(8,128)(2,1)S(1)}) fusion(bf16[2,256,1024]{2,1,0:T(8,128)(2,1)} %collective-permute-done, s32[]{:T(128)S(6)} %select_n.22, bf16[2,256,1024]{2,1,0:T(8,128)(2,1)S(1)} %get-tuple-element.58, s32[]{:T(128)S(6)} %select_n.21), kind=kLoop, calls=%fused_computation | loop fusion | flops 524288 | bytes 3145736 | tf_op jit(solution)/shard_map/add | solution.py:406
  19.7 4.3 %collective-permute-start.1 = (bf16[256,1024]{1,0:T(8,128)(2,1)S(1)}, bf16[256,1024]{1,0:T(8,128)(2,1)S(1)}, u32[]{:S(2)}, u32[]{:S(2)}) collective-permute-start(bf16[256,1024]{1,0:T(8,128)(2,1)S(1)} %get-tuple-element.104), channel_id=1, source_target_pairs={{0,2},{1,3},{2,0},{3,1},{4,6},{5,7},{6,4},{7,5},{8,10},{9,11},{10,... | collective-permute-start | bytes 1572872 | tf_op jit(solution)/shard_map/ppermute | solution.py:370
  24.0 8.4 %base_terms.5.refs_0_ = bf16[256,1024]{1,0:T(8,128)(2,1)S(1)} custom-call(s32[38]{0:T(128)S(1)} %copy-done.4, bf16[1024,7168]{1,0:T(8,128)(2,1)} %refs_1_.5, bf16[7168,2048]{1,0:T(8,128)(2,1)} %refs_2_.7), custom_call_target="tpu_custom_call" | custom-call | flops 1000000 | bytes 100000 | tf_op jit(solution)/shard_map/base_terms/pallas_call | solution.py:220
  32.4 3.9 %collective-permute-done.1 = bf16[256,1024]{1,0:T(8,128)(2,1)S(1)} collective-permute-done((bf16[256,1024]{1,0:T(8,128)(2,1)S(1)}, bf16[256,1024]{1,0:T(8,128)(2,1)S(1)}, u32[]{:S(2)}, u32[]{:S(2)}) %collective-permute-start.1) | collective-permute-done | bytes 524320 | tf_op jit(solution)/shard_map/ppermute | solution.py:370
  36.3 0.2 add.51.refs_2_.refs_5_
  36.7 0.7 collective-permute-start.5
  37.4 4.3 %collective-permute-start.3 = (bf16[256,1024]{1,0:T(8,128)(2,1)S(1)}, bf16[256,1024]{1,0:T(8,128)(2,1)S(1)}, u32[]{:S(2)}, u32[]{:S(2)}) collective-permute-start(bf16[256,1024]{1,0:T(8,128)(2,1)S(1)} %base_terms.5.refs_0_), channel_id=1, source_target_pairs={{0,4},{12,8},{1,5},{13,9},{2,6},{14,10},{3,7},{15,11},{16,20},{28,... | collective-permute-start | bytes 1572872 | tf_op jit(solution)/shard_map/ppermute | solution.py:379
  41.9 16.5 %base_terms.6 = (bf16[576,1024]{1,0:T(8,128)(2,1)S(1)}, bf16[288,1024]{1,0:T(8,128)(2,1)S(1)}) custom-call(s32[38]{0:T(128)S(1)} %copy-done.4, s32[8,128]{1,0:T(8,128)S(1)} %bitcast.17, bf16[4,7168,128]{2,1,0:T(8,128)(2,1)S(1)} %bitcast.15, bf16[1024,7168]{1,0:T(8,128)(2,1)} %refs_1_.5, bf16[7168,2048]{1,0:T(8,128)(2,1)} %refs_2_.7), custom_call_target="tpu_custom_call" | custom-call | flops 1000000 | bytes 100000 | tf_op jit(solution)/shard_map/base_terms/pallas_call | solution.py:220
  58.4 4.0 %collective-permute-start.6 = (bf16[576,1024]{1,0:T(8,128)(2,1)S(1)}, bf16[576,1024]{1,0:T(8,128)(2,1)S(1)}, u32[]{:S(2)}, u32[]{:S(2)}) collective-permute-start(bf16[576,1024]{1,0:T(8,128)(2,1)S(1)} %get-tuple-element.84.refs_0_), channel_id=1, source_target_pairs={{0,4},{12,8},{1,5},{13,9},{2,6},{14,10},{3,7},{15,11},{16,20},{28,... | collective-permute-start | bytes 3538952 | tf_op jit(solution)/shard_map/ppermute | solution.py:379
  62.4 2.9 %collective-permute-done.4.refs_2_.refs_6_ = bf16[256,1024]{1,0:T(8,128)(2,1)S(1)} collective-permute-done((bf16[256,1024]{1,0:T(8,128)(2,1)S(1)}, bf16[256,1024]{1,0:T(8,128)(2,1)S(1)}, u32[]{:S(2)}, u32[]{:S(2)}) %collective-permute-start.4) | collective-permute-done | bytes 524320 | tf_op jit(solution)/shard_map/ppermute | solution.py:416
  65.6 1.3 %collective-permute-start.8 = (bf16[544,1024]{1,0:T(8,128)(2,1)S(1)}, bf16[544,1024]{1,0:T(8,128)(2,1)S(1)}, u32[]{:S(2)}, u32[]{:S(2)}) collective-permute-start(bf16[544,1024]{1,0:T(8,128)(2,1)S(1)} %join.8), channel_id=1, source_target_pairs={{8,12},{4,0},{9,13},{5,1},{10,14},{6,2},{11,15},{7,3},{24,28},{20,... | collective-permute-start | bytes 3342344 | tf_op jit(solution)/shard_map/ppermute | solution.py:379
  66.9 0.7 collective-permute-start.7
  67.7 15.6 %base_terms.7 = (bf16[256,1024]{1,0:T(8,128)(2,1)S(1)}, bf16[256,1024]{1,0:T(8,128)(2,1)S(1)}, bf16[256,1024]{1,0:T(8,128)(2,1)S(1)}) custom-call(s32[38]{0:T(128)S(1)} %copy-done.4, bf16[1024,7168]{1,0:T(8,128)(2,1)} %refs_1_.5, bf16[7168,2048]{1,0:T(8,128)(2,1)} %refs_2_.7), custom_call_target="tpu_custom_call" | custom-call | flops 1000000 | bytes 100000 | tf_op jit(solution)/shard_map/base_terms/pallas_call | solution.py:220
  83.3 5.9 %collective-permute-done.6.refs_1_.refs_11_ = bf16[576,1024]{1,0:T(8,128)(2,1)S(1)} collective-permute-done((bf16[576,1024]{1,0:T(8,128)(2,1)S(1)}, bf16[576,1024]{1,0:T(8,128)(2,1)S(1)}, u32[]{:S(2)}, u32[]{:S(2)}) %collective-permute-start.6) | collective-permute-done | bytes 1179680 | tf_op jit(solution)/shard_map/ppermute | solution.py:379
  89.4 0.7 collective-permute-start.10
  90.1 6.0 %collective-permute-start.9 = (bf16[256,1024]{1,0:T(8,128)(2,1)S(1)}, bf16[256,1024]{1,0:T(8,128)(2,1)S(1)}, u32[]{:S(2)}, u32[]{:S(2)}) collective-permute-start(bf16[256,1024]{1,0:T(8,128)(2,1)S(1)} %get-tuple-element.96.refs_0_), channel_id=1, source_target_pairs={{0,4},{12,8},{1,5},{13,9},{2,6},{14,10},{3,7},{15,11},{16,20},{28,... | collective-permute-start | bytes 1572872 | tf_op jit(solution)/shard_map/ppermute | solution.py:379
  96.3 1.3 %collective-permute-start.13 = (bf16[512,1024]{1,0:T(8,128)(2,1)S(1)}, bf16[512,1024]{1,0:T(8,128)(2,1)S(1)}, u32[]{:S(2)}, u32[]{:S(2)}) collective-permute-start(bf16[512,1024]{1,0:T(8,128)(2,1)S(1)} %join.10), channel_id=1, source_target_pairs={{8,12},{4,0},{9,13},{5,1},{10,14},{6,2},{11,15},{7,3},{24,28},{20,... | collective-permute-start | bytes 3145736 | tf_op jit(solution)/shard_map/ppermute | solution.py:379
  97.6 8.3 %collective-permute-done.9.refs_1_ = bf16[256,1024]{1,0:T(8,128)(2,1)S(1)} collective-permute-done((bf16[256,1024]{1,0:T(8,128)(2,1)S(1)}, bf16[256,1024]{1,0:T(8,128)(2,1)S(1)}, u32[]{:S(2)}, u32[]{:S(2)}) %collective-permute-start.9) | collective-permute-done | bytes 524320 | tf_op jit(solution)/shard_map/ppermute | solution.py:379
  106.0 0.7 collective-permute-start.15
  106.7 7.3 %collective-permute-start.14 = (bf16[256,1024]{1,0:T(8,128)(2,1)S(1)}, bf16[256,1024]{1,0:T(8,128)(2,1)S(1)}, u32[]{:S(2)}, u32[]{:S(2)}) collective-permute-start(bf16[256,1024]{1,0:T(8,128)(2,1)S(1)} %get-tuple-element.102.refs_0_), channel_id=1, source_target_pairs={{0,4},{12,8},{1,5},{13,9},{2,6},{14,10},{3,7},{15,11},{16,20},{28,... | collective-permute-start | bytes 1572872 | tf_op jit(solution)/shard_map/ppermute | solution.py:379
  114.2 1.2 collective-permute-done.11
  115.4 1.3 %collective-permute-start.12 = (bf16[256,128]{1,0:T(8,128)(2,1)S(1)}, bf16[256,128]{1,0:T(8,128)(2,1)S(1)}, u32[]{:S(2)}, u32[]{:S(2)}) collective-permute-start(bf16[256,128]{1,0:T(8,128)(2,1)S(1)} %bitcast_add_fusion), channel_id=1, source_target_pairs={{0,2},{1,3},{2,0},{3,1},{4,6},{5,7},{6,4},{7,5},{8,10},{9,11},{10,... | collective-permute-start | bytes 196616 | tf_op jit(solution)/shard_map/ppermute | solution.py:370
  116.7 3.1 %collective-permute-done.12 = bf16[256,128]{1,0:T(8,128)(2,1)S(1)} collective-permute-done((bf16[256,128]{1,0:T(8,128)(2,1)S(1)}, bf16[256,128]{1,0:T(8,128)(2,1)S(1)}, u32[]{:S(2)}, u32[]{:S(2)}) %collective-permute-start.12) | collective-permute-done | bytes 65568 | tf_op jit(solution)/shard_map/ppermute | solution.py:370
  119.8 1.6 %collective-permute-done.13.refs_10_ = bf16[512,1024]{1,0:T(8,128)(2,1)S(1)} collective-permute-done((bf16[512,1024]{1,0:T(8,128)(2,1)S(1)}, bf16[512,1024]{1,0:T(8,128)(2,1)S(1)}, u32[]{:S(2)}, u32[]{:S(2)}) %collective-permute-start.13) | collective-permute-done | bytes 1048608 | tf_op jit(solution)/shard_map/ppermute | solution.py:379
  121.4 1.8 %finish.1.total = bf16[256,2048]{1,0:T(8,128)(2,1)S(1)} custom-call(s32[38]{0:T(128)S(1)} %copy-done.4, s32[8,128]{1,0:T(8,128)S(1)} %bitcast.18, bf16[256,128]{1,0:T(8,128)(2,1)S(1)} %add.56.refs_2_, bf16[288,1024]{1,0:T(8,128)(2,1)S(1)} %get-tuple-element.99.refs_3_, bf16[256,1024]{1,0:T(8,128)(2,1)S(1)} %get-tuple-element.101.refs_4_, ...), custom_call_target="tpu_custom_call" | custom-call | flops 1000000 | bytes 100000 | tf_op jit(solution)/shard_map/finish/pallas_call | solution.py:312
  123.2 1.2 add_last.1
  (36 shorter events, 1.1 us)
Async XLA Ops:
  0.8 1.6 %copy-start.1 = (bf16[4,32,8192]{2,1,0:T(8,128)(2,1)S(1)}, bf16[4,32,8192]{2,1,0:T(8,128)(2,1)}, u32[]{:S(2)}) copy-start(bf16[4,32,8192]{2,1,0:T(8,128)(2,1)} %refs_1_.3) | copy-start | bytes 6291460
  2.4 2.2 %copy-start.3 = (s32[38]{0:T(128)}, s32[38]{0:T(128)S(1)}, u32[]{:S(2)}) copy-start(s32[38]{0:T(128)S(1)} %concatenate.3.refs_0_) | copy-start | bytes 460
  4.1 14.3 %collective-permute-start = (bf16[2,256,1024]{2,1,0:T(8,128)(2,1)}, bf16[2,256,1024]{2,1,0:T(8,128)(2,1)}, u32[]{:S(2)}, u32[]{:S(2)}) collective-permute-start(bf16[2,256,1024]{2,1,0:T(8,128)(2,1)} %get-tuple-element.55), channel_id=1, source_target_pairs={{0,1},{1,0},{2,3},{3,2},{4,5},{5,4},{6,7},{7,6},{8,9},{9,8},{10,11... | collective-permute-start | bytes 3145736 | tf_op jit(solution)/shard_map/ppermute | solution.py:370
  13.9 22.7 %collective-permute-start.2 = (bf16[288,1024]{1,0:T(8,128)(2,1)}, bf16[288,1024]{1,0:T(8,128)(2,1)S(1)}, u32[]{:S(2)}, u32[]{:S(2)}) collective-permute-start(bf16[288,1024]{1,0:T(8,128)(2,1)} %base_terms.4.refs_0_), channel_id=1, source_target_pairs={{0,4},{12,8},{1,5},{13,9},{2,6},{14,10},{3,7},{15,11},{16,20},{28,... | collective-permute-start | bytes 1769480 | tf_op jit(solution)/shard_map/ppermute | solution.py:379
  18.4 5.6 %copy-start.4 = (s32[38]{0:T(128)S(1)}, s32[38]{0:T(128)}, u32[]{:S(2)}) copy-start(s32[38]{0:T(128)} %copy-done.3) | copy-start | bytes 460
  19.7 16.6 %collective-permute-start.1 = (bf16[256,1024]{1,0:T(8,128)(2,1)S(1)}, bf16[256,1024]{1,0:T(8,128)(2,1)S(1)}, u32[]{:S(2)}, u32[]{:S(2)}) collective-permute-start(bf16[256,1024]{1,0:T(8,128)(2,1)S(1)} %get-tuple-element.104), channel_id=1, source_target_pairs={{0,2},{1,3},{2,0},{3,1},{4,6},{5,7},{6,4},{7,5},{8,10},{9,11},{10,... | collective-permute-start | bytes 1572872 | tf_op jit(solution)/shard_map/ppermute | solution.py:370
  24.0 17.9 %slice-start = ((s8[7340032]{0:T(1024)(128)(4,1)}), s8[4194304]{0:T(1024)(128)(4,1)S(1)}, s32[]{:S(2)}) async-start(s8[7340032]{0:T(1024)(128)(4,1)} %bitcast.14), calls=%async_computation | async-start | bytes 8388608
  24.0 17.9 %slice-start.1 = ((s8[7340032]{0:T(1024)(128)(4,1)}), s8[3145728]{0:T(1024)(128)(4,1)S(1)}, s32[]{:S(2)}) async-start(s8[7340032]{0:T(1024)(128)(4,1)} %bitcast.14), calls=%async_computation.1 | async-start | bytes 6291456
  32.4 4.1 %copy-start = (bf16[288,1024]{1,0:T(8,128)(2,1)S(1)}, bf16[288,1024]{1,0:T(8,128)(2,1)}, u32[]{:S(2)}) copy-start(bf16[288,1024]{1,0:T(8,128)(2,1)} %base_terms.4.refs_0_) | copy-start | bytes 1769476
  36.5 5.4 %copy-start.2 = (s32[1024]{0:T(1024)S(1)}, s32[1024]{0:T(1024)}, u32[]{:S(2)}) copy-start(s32[1024]{0:T(1024)} %param.12) | copy-start | bytes 12292
  36.7 28.8 %collective-permute-start.5 = (bf16[544,1024]{1,0:T(8,128)(2,1)S(1)}, bf16[544,1024]{1,0:T(8,128)(2,1)S(1)}, u32[]{:S(2)}, u32[]{:S(2)}) collective-permute-start(bf16[544,1024]{1,0:T(8,128)(2,1)S(1)} %join.6), channel_id=1, source_target_pairs={{4,8},{8,4},{5,9},{9,5},{6,10},{10,6},{7,11},{11,7},{20,24},{24,20... | collective-permute-start | bytes 3342344 | tf_op jit(solution)/shard_map/ppermute | solution.py:379
  37.4 25.0 %collective-permute-start.3 = (bf16[256,1024]{1,0:T(8,128)(2,1)S(1)}, bf16[256,1024]{1,0:T(8,128)(2,1)S(1)}, u32[]{:S(2)}, u32[]{:S(2)}) collective-permute-start(bf16[256,1024]{1,0:T(8,128)(2,1)S(1)} %base_terms.5.refs_0_), channel_id=1, source_target_pairs={{0,4},{12,8},{1,5},{13,9},{2,6},{14,10},{3,7},{15,11},{16,20},{28,... | collective-permute-start | bytes 1572872 | tf_op jit(solution)/shard_map/ppermute | solution.py:379
  41.8 23.5 %collective-permute-start.4 = (bf16[256,1024]{1,0:T(8,128)(2,1)S(1)}, bf16[256,1024]{1,0:T(8,128)(2,1)S(1)}, u32[]{:S(2)}, u32[]{:S(2)}) collective-permute-start(bf16[256,1024]{1,0:T(8,128)(2,1)S(1)} %add.51.refs_2_.refs_5_), channel_id=1, source_target_pairs={{0,4},{12,8},{4,0},{8,12},{1,5},{13,9},{5,1},{9,13},{2,6},{14,10},... | collective-permute-start | bytes 1572872 | tf_op jit(solution)/shard_map/ppermute | solution.py:416
  58.4 30.8 %collective-permute-start.6 = (bf16[576,1024]{1,0:T(8,128)(2,1)S(1)}, bf16[576,1024]{1,0:T(8,128)(2,1)S(1)}, u32[]{:S(2)}, u32[]{:S(2)}) collective-permute-start(bf16[576,1024]{1,0:T(8,128)(2,1)S(1)} %get-tuple-element.84.refs_0_), channel_id=1, source_target_pairs={{0,4},{12,8},{1,5},{13,9},{2,6},{14,10},{3,7},{15,11},{16,20},{28,... | collective-permute-start | bytes 3538952 | tf_op jit(solution)/shard_map/ppermute | solution.py:379
  65.6 30.5 %collective-permute-start.8 = (bf16[544,1024]{1,0:T(8,128)(2,1)S(1)}, bf16[544,1024]{1,0:T(8,128)(2,1)S(1)}, u32[]{:S(2)}, u32[]{:S(2)}) collective-permute-start(bf16[544,1024]{1,0:T(8,128)(2,1)S(1)} %join.8), channel_id=1, source_target_pairs={{8,12},{4,0},{9,13},{5,1},{10,14},{6,2},{11,15},{7,3},{24,28},{20,... | collective-permute-start | bytes 3342344 | tf_op jit(solution)/shard_map/ppermute | solution.py:379
  66.9 29.2 %collective-permute-start.7 = (bf16[512,1024]{1,0:T(8,128)(2,1)S(1)}, bf16[512,1024]{1,0:T(8,128)(2,1)S(1)}, u32[]{:S(2)}, u32[]{:S(2)}) collective-permute-start(bf16[512,1024]{1,0:T(8,128)(2,1)S(1)} %join.7), channel_id=1, source_target_pairs={{4,8},{8,4},{5,9},{9,5},{6,10},{10,6},{7,11},{11,7},{20,24},{24,20... | collective-permute-start | bytes 3145736 | tf_op jit(solution)/shard_map/ppermute | solution.py:379
  89.4 17.3 %collective-permute-start.10 = (bf16[288,1024]{1,0:T(8,128)(2,1)S(1)}, bf16[288,1024]{1,0:T(8,128)(2,1)S(1)}, u32[]{:S(2)}, u32[]{:S(2)}) collective-permute-start(bf16[288,1024]{1,0:T(8,128)(2,1)S(1)} %join.9), channel_id=1, source_target_pairs={{4,8},{8,4},{5,9},{9,5},{6,10},{10,6},{7,11},{11,7},{20,24},{24,20... | collective-permute-start | bytes 1769480 | tf_op jit(solution)/shard_map/ppermute | solution.py:379
  90.1 15.8 %collective-permute-start.9 = (bf16[256,1024]{1,0:T(8,128)(2,1)S(1)}, bf16[256,1024]{1,0:T(8,128)(2,1)S(1)}, u32[]{:S(2)}, u32[]{:S(2)}) collective-permute-start(bf16[256,1024]{1,0:T(8,128)(2,1)S(1)} %get-tuple-element.96.refs_0_), channel_id=1, source_target_pairs={{0,4},{12,8},{1,5},{13,9},{2,6},{14,10},{3,7},{15,11},{16,20},{28,... | collective-permute-start | bytes 1572872 | tf_op jit(solution)/shard_map/ppermute | solution.py:379
  96.3 25.1 %collective-permute-start.13 = (bf16[512,1024]{1,0:T(8,128)(2,1)S(1)}, bf16[512,1024]{1,0:T(8,128)(2,1)S(1)}, u32[]{:S(2)}, u32[]{:S(2)}) collective-permute-start(bf16[512,1024]{1,0:T(8,128)(2,1)S(1)} %join.10), channel_id=1, source_target_pairs={{8,12},{4,0},{9,13},{5,1},{10,14},{6,2},{11,15},{7,3},{24,28},{20,... | collective-permute-start | bytes 3145736 | tf_op jit(solution)/shard_map/ppermute | solution.py:379
  106.0 17.2 %collective-permute-start.15 = (bf16[256,1024]{1,0:T(8,128)(2,1)S(1)}, bf16[256,1024]{1,0:T(8,128)(2,1)S(1)}, u32[]{:S(2)}, u32[]{:S(2)}) collective-permute-start(bf16[256,1024]{1,0:T(8,128)(2,1)S(1)} %join.11), channel_id=1, source_target_pairs={{4,8},{8,4},{5,9},{9,5},{6,10},{10,6},{7,11},{11,7},{20,24},{24,20... | collective-permute-start | bytes 1572872 | tf_op jit(solution)/shard_map/ppermute | solution.py:379
  106.7 16.5 %collective-permute-start.14 = (bf16[256,1024]{1,0:T(8,128)(2,1)S(1)}, bf16[256,1024]{1,0:T(8,128)(2,1)S(1)}, u32[]{:S(2)}, u32[]{:S(2)}) collective-permute-start(bf16[256,1024]{1,0:T(8,128)(2,1)S(1)} %get-tuple-element.102.refs_0_), channel_id=1, source_target_pairs={{0,4},{12,8},{1,5},{13,9},{2,6},{14,10},{3,7},{15,11},{16,20},{28,... | collective-permute-start | bytes 1572872 | tf_op jit(solution)/shard_map/ppermute | solution.py:379
  114.1 1.3 %collective-permute-start.11 = (bf16[256,128]{1,0:T(8,128)(2,1)S(1)}, bf16[256,128]{1,0:T(8,128)(2,1)S(1)}, u32[]{:S(2)}, u32[]{:S(2)}) collective-permute-start(bf16[256,128]{1,0:T(8,128)(2,1)S(1)} %bitcast.19), channel_id=1, source_target_pairs={{0,1},{1,0},{2,3},{3,2},{4,5},{5,4},{6,7},{7,6},{8,9},{9,8},{10,11... | collective-permute-start | bytes 196616 | tf_op jit(solution)/shard_map/ppermute | solution.py:370
  115.4 4.3 %collective-permute-start.12 = (bf16[256,128]{1,0:T(8,128)(2,1)S(1)}, bf16[256,128]{1,0:T(8,128)(2,1)S(1)}, u32[]{:S(2)}, u32[]{:S(2)}) collective-permute-start(bf16[256,128]{1,0:T(8,128)(2,1)S(1)} %bitcast_add_fusion), channel_id=1, source_target_pairs={{0,2},{1,3},{2,0},{3,1},{4,6},{5,7},{6,4},{7,5},{8,10},{9,11},{10,... | collective-permute-start | bytes 196616 | tf_op jit(solution)/shard_map/ppermute | solution.py:370
